TPU v7x, 512 devices: a whole 4x4x16 slice. The times are simulated.
512 devices in a mesh: traj: 32 (over z_hi, y, core), tm: 16 (over z_lo, x).
Axes of the slice: x: 4, y: 4, z: 16 (z_hi: 4, z_lo: 4; z = z_hi * 4 + z_lo), core: 2. Of those that a mesh axis runs over, the one named last changes fastest.
Arguments:
- states: float32 [16, 32, 8192], P('tm', None, 'traj'), may hold values from -6 to 6
- vectors: bfloat16 [64, 8192], P(None, 'traj'), may hold values from -6 to 6
- kernel_scale: float32 [16], P('tm'), may hold values from 6 to 16
- neighbour_blocks: int32 [64, 24], P('traj'), may hold values from 0 to 63, as said below
- neighbour_count: int32 [64], P('traj'), may hold values from 6 to 24, as said below
Outputs:
- result: float32 [64, 8192], P(None, 'traj')
Inputs may be any that keep to these rules, and one draw needn't show every extreme that they name: `neighbour_blocks`: row b names 24 different blocks, the first of them b itself. Only the first neighbour_count[b] entries of row b of neighbour_blocks are neighbours of block b; some block uses all 24.
All inputs are finite; a program needn't handle non-finite values.
Results may differ from a plain program's by a relative error of at most 0.0013.
Values may be sent and summed in bfloat16 or wider, within the bound.
A program may use at most 64 MiB of HBM per device.

v0:
```python
import math
import jax
import jax.numpy as jnp
from jax import lax
from jax.sharding import Mesh
from jax.sharding import PartitionSpec as P

BLK = 128
TRAJ = ("traj_0", "traj_1", "traj_2")


def in_order(blocks, dim):
    dims = list(blocks.shape[1:])
    dims[dim] *= blocks.shape[0]
    return jnp.moveaxis(blocks, 0, dim).reshape(dims)


def all_blocks(array, axes, turns):
    blocks = array[None]
    for k in turns:
        blocks = lax.all_gather(blocks, axes[k], axis=0, tiled=True)
    block = [lax.axis_size(axes[k]) for k in reversed(turns)]
    blocks = blocks.reshape(*block, *array.shape)
    turned = sorted(range(len(turns)), key=lambda place: turns[len(turns) - 1 - place])
    return blocks.transpose(*turned, *range(len(turns), blocks.ndim)).reshape(-1, *array.shape)


def gather_axes(array, axes, turns, dim):
    return in_order(all_blocks(array, axes, turns), dim)


def sent_together(arrays, axis, dim, along):
    widths = [math.prod(a.shape[along:]) for a in arrays]
    both = jnp.concatenate(
        [a.reshape(*a.shape[:along], w) for a, w in zip(arrays, widths)], axis=along
    )
    out = lax.all_gather(both, axis, axis=dim, tiled=True)
    blocks = jnp.split(out, [sum(widths[:k]) for k in range(1, len(widths))], axis=along)
    return tuple((b.reshape(*out.shape[:along], *a.shape[along:]) for a, b in zip(arrays, blocks)))


def copy_for_each(array, axis):
    copies = jnp.broadcast_to(array, (lax.axis_size(axis), *array.shape))
    return lax.all_to_all(copies, axis, split_axis=0, concat_axis=0, tiled=True)


def of_everyone(array, axis):
    return copy_for_each(array, axis).sum(axis=0)


def linked_blocks(neighbour_blocks, neighbour_count, blocks_total):
    slots = neighbour_blocks.shape[1]
    named = neighbour_blocks[:, :, None] == jnp.arange(blocks_total, dtype=jnp.int32)[None, None, :]
    within = jnp.arange(slots, dtype=jnp.int32)[None, :, None] < neighbour_count[:, None, None]
    return jnp.any(named & within, axis=1).astype(jnp.float32)


def per_device(states, vectors, kernel_scale, neighbour_blocks, neighbour_count):
    coords_all = gather_axes(states, (("traj_0", "traj_1"), "traj_2"), (0, 1), 2)[0]
    vectors_all = lax.all_gather(vectors, TRAJ, axis=1, tiled=True)
    own = states[0]
    spread = kernel_scale[0]
    own_rows = own.shape[1]
    columns = coords_all.shape[1]
    vector_count = vectors.shape[0]
    blocks_total = columns // BLK
    block_rows = own_rows // BLK
    own_squares = jnp.sum(own * own, axis=0)
    all_squares = jnp.sum(coords_all * coords_all, axis=0)
    tile_width = math.gcd(columns, 512)
    tile_count = columns // tile_width
    linked = linked_blocks(neighbour_blocks, neighbour_count, blocks_total)

    def dense_kernel(tile_index):
        offset = tile_index * tile_width
        slab = lax.dynamic_slice_in_dim(coords_all, offset, tile_width, 1)
        cross = lax.dot_general(
            own, slab, (((0,), (0,)), ((), ())), precision=lax.Precision.HIGHEST
        )
        slab_squares = lax.dynamic_slice_in_dim(all_squares, offset, tile_width, 0)
        distance = own_squares[:, None] + slab_squares[None, :] - 2.0 * cross
        mask = lax.dynamic_slice_in_dim(linked, offset // BLK, tile_width // BLK, 1)
        shaped = jnp.exp(-distance / spread).reshape(block_rows, BLK, tile_width // BLK, BLK)
        return (mask[:, None, :, None] * shaped).reshape(own_rows, tile_width)

    def first_dense(tile_index, carry):
        row_sum, pushed = carry
        kernel = dense_kernel(tile_index)
        weights = kernel.astype(jnp.bfloat16)
        slab_vectors = lax.dynamic_slice_in_dim(vectors_all, tile_index * tile_width, tile_width, 1)
        pushed = pushed + lax.dot_general(
            slab_vectors, weights, (((1,), (1,)), ((), ())), preferred_element_type=jnp.float32
        )
        return (row_sum + jnp.sum(kernel, axis=1), pushed)

    row_sum, pushed = lax.fori_loop(
        0,
        tile_count,
        first_dense,
        (jnp.zeros((own_rows,), jnp.float32), jnp.zeros((vector_count, own_rows), jnp.float32)),
    )
    scaled = (pushed / (row_sum * row_sum)[None, :]).astype(jnp.bfloat16)
    lists_whole, counts_whole = sent_together((neighbour_blocks, neighbour_count), TRAJ, 0, 1)
    linked_whole = linked_blocks(lists_whole, counts_whole, blocks_total)
    own_start = lax.axis_index(TRAJ) * block_rows
    column_mask = lax.dynamic_slice_in_dim(linked_whole, own_start, block_rows, 1)
    scaled_whole = lax.all_gather(scaled, TRAJ, axis=1, tiled=True)

    def pull_tile(tile_index, total):
        offset = tile_index * tile_width
        slab = lax.dynamic_slice_in_dim(coords_all, offset, tile_width, 1)
        cross = lax.dot_general(
            slab, own, (((0,), (0,)), ((), ())), precision=lax.Precision.HIGHEST
        )
        slab_squares = lax.dynamic_slice_in_dim(all_squares, offset, tile_width, 0)
        distance = slab_squares[:, None] + own_squares[None, :] - 2.0 * cross
        mask = lax.dynamic_slice_in_dim(column_mask, offset // BLK, tile_width // BLK, 0)
        shaped = jnp.exp(-distance / spread).reshape(tile_width // BLK, BLK, block_rows, BLK)
        weights = (
            (mask[:, None, :, None] * shaped).reshape(tile_width, own_rows).astype(jnp.bfloat16)
        )
        slab_scaled = lax.dynamic_slice_in_dim(scaled_whole, offset, tile_width, 1)
        return total + jnp.dot(slab_scaled, weights, preferred_element_type=jnp.float32)

    own_pulled = lax.fori_loop(
        0, tile_count, pull_tile, jnp.zeros((vector_count, own_rows), jnp.float32)
    )
    result = of_everyone(own_pulled, "tm")
    return result


def solution(mesh):
    split = Mesh(
        mesh.devices.reshape(4, 4, 2, mesh.shape["tm"]), ("traj_0", "traj_1", "traj_2", "tm")
    )
    in_specs = (P("tm", None, TRAJ), P(None, TRAJ), P("tm"), P(TRAJ, None), P(TRAJ))
    out_specs = P(None, TRAJ)
    return jax.shard_map(
        per_device, mesh=split, in_specs=in_specs, out_specs=out_specs, check_vma=False
    )
```

profile of v0, /device:TPU:8, one launch (start us, length us, event | category | flops | bytes accessed | tf_op | source)
XLA Modules:
  0.0 365.6 jit_solution(11835117052081428395)
XLA Ops:
  6.5 60.4 %all-gather = f32[16,32,256]{2,1,0:T(8,128)} all-gather(f32[1,32,256]{2,1,0:T(8,128)} %param.9), channel_id=2, replica_groups=mesh['traj_0'=4,'traj_1'=4,'traj_2'=2,'tm'=16] {'traj_0','traj_1'}, dimensions={0}, use_global_device_ids=true | all-gather | bytes 557056 | tf_op jit(solution)/shard_map/all_gather | solution.py:21
  69.3 16.1 %all-gather.11.cloned.1.call-done = f32[32,32,256]{2,1,0:T(8,128)} async-done(((f32[16,32,256]{2,1,0:T(8,128)}), f32[32,32,256]{2,1,0:T(8,128)}) %all-gather.11.cloned.1.call-update) | async-done | bytes 1048592 | tf_op jit(solution)/shard_map/all_gather | solution.py:21
  85.4 1.3 copy.19
  87.0 74.4 %all-gather.7.cloned.1.call-done = bf16[64,8192]{1,0:T(8,128)(2,1)} async-done(((bf16[64,256]{1,0:T(8,128)(2,1)}), bf16[64,8192]{1,0:T(8,128)(2,1)}) %all-gather.7.cloned.1.call-update) | async-done | bytes 1048592 | tf_op jit(solution)/shard_map/all_gather | solution.py:60
  161.4 47.5 %while.34 = (s32[]{:T(128)}, f32[256]{0:T(256)S(1)}, f32[64,256]{1,0:T(8,128)S(1)}, f32[2,64]{1,0:T(2,128)S(1)}, f32[256]{0:T(256)S(1)}, /*index=5*/f32[8192]{0:...) while((s32[]{:T(128)}, f32[256]{0:T(256)S(1)}, ...), condition=%wide.region_6.7_spmd.clone, body=%wide.region_4.0_spmd.clone.sunk | while | flops 68190488 | bytes 1879617 | solution.py:96
  161.9 1.4 fusion.42
  163.3 1.0 convolution_add_fusion.4
  164.9 1.4 fusion.42
  166.3 1.0 convolution_add_fusion.4
  167.8 1.4 fusion.42
  169.2 1.0 convolution_add_fusion.4
  170.8 1.4 fusion.42
  172.2 1.0 convolution_add_fusion.4
  173.8 1.4 fusion.42
  175.2 1.0 convolution_add_fusion.4
  176.8 1.4 fusion.42
  178.2 1.0 convolution_add_fusion.4
  179.7 1.4 fusion.42
  181.1 1.0 convolution_add_fusion.4
  182.7 1.4 fusion.42
  184.1 1.0 convolution_add_fusion.4
  185.7 1.4 fusion.42
  187.1 1.0 convolution_add_fusion.4
  188.6 1.4 fusion.42
  190.0 1.0 convolution_add_fusion.4
  191.6 1.4 fusion.42
  193.0 1.0 convolution_add_fusion.4
  194.6 1.4 fusion.42
  196.0 1.0 convolution_add_fusion.4
  197.6 1.4 fusion.42
  199.0 1.0 convolution_add_fusion.4
  200.5 1.4 fusion.42
  201.9 1.0 convolution_add_fusion.4
  203.5 1.4 fusion.42
  204.9 1.0 convolution_add_fusion.4
  206.5 1.4 fusion.42
  207.9 1.0 convolution_add_fusion.4
  209.8 47.4 %all-gather.2 = s32[32,2,25]{2,1,0:T(2,128)S(1)} all-gather(s32[1,2,25]{2,1,0:T(2,128)S(1)} %add_bitcast_fusion), channel_id=1, replica_groups=mesh['traj_0'=4,'traj_1'=4,'traj_2'=2,'tm'=16] {'traj_0','traj_1','traj_2'}, dimensions={0}, use_global_device_ids=true | all-gather | bytes 6600 | tf_op jit(solution)/shard_map/all_gather | solution.py:37
  258.1 20.6 %all-gather.9.cloned.1.call-done = bf16[64,8192]{1,0:T(8,128)(2,1)} async-done(((bf16[64,256]{1,0:T(8,128)(2,1)}), bf16[64,8192]{1,0:T(8,128)(2,1)}) %all-gather.9.cloned.1.call-update) | async-done | bytes 1048592 | tf_op jit(solution)/shard_map/all_gather | solution.py:107
  278.7 44.3 %while.35 = (s32[]{:T(128)}, f32[64,256]{1,0:T(8,128)S(1)}, bf16[64,8192]{1,0:T(8,128)(2,1)}, f32[64,2]{1,0:T(8,128)S(1)}, f32[8192]{0:T(1024)S(1)}, /*index=5*/...) while((s32[]{:T(128)}, f32[64,256]{1,0:T(8,128)S(1)}, ...), condition=%wide.region_8.9_spmd.clone, body=%wide.region_7.8_spmd.clone.sunk | while | flops 68059160 | bytes 1875448 | solution.py:125
  279.0 1.4 fusion.47
  280.4 1.0 convolution_add_fusion.5
  281.8 1.4 fusion.47
  284.6 1.4 fusion.47
  286.0 1.0 convolution_add_fusion.5
  287.4 1.4 fusion.47
  288.7 1.0 convolution_add_fusion.5
  290.1 1.4 fusion.47
  291.5 1.0 convolution_add_fusion.5
  292.9 1.4 fusion.47
  295.7 1.4 fusion.47
  298.4 1.4 fusion.47
  299.8 1.0 convolution_add_fusion.5
  301.2 1.4 fusion.47
  304.0 1.4 fusion.47
  306.8 1.4 fusion.47
  308.1 1.0 convolution_add_fusion.5
  309.5 1.4 fusion.47
  312.3 1.4 fusion.47
  315.1 1.4 fusion.47
  316.5 1.0 convolution_add_fusion.5
  317.9 1.4 fusion.47
  320.6 1.4 fusion.47
  323.2 35.2 %all_to_all.5 = f32[16,64,256]{2,1,0:T(8,128)S(1)} all-to-all(f32[16,64,256]{2,1,0:T(8,128)S(1)} %broadcast_in_dim.37), channel_id=1, replica_groups=mesh['traj_0'=4,'traj_1'=4,'traj_2'=2,'tm'=16] {'tm'}, dimensions={0} | all-to-all | bytes 2097152 | tf_op jit(solution)/shard_map/all_to_all | solution.py:44
  (170 shorter events, 26.4 us)
Async XLA Ops:
  6.5 78.9 %all-gather.11.cloned.1.call-start = ((), (), s32[]{:S(2)}) async-start(), calls=%async_computation.3 | async-start | bytes 1572864 | tf_op jit(solution)/shard_map/all_gather | solution.py:21
  67.0 2.3 copy-start
  67.0 94.4 %all-gather.7.cloned.1.call-start = ((), (), s32[]{:S(2)}) async-start(), calls=%async_computation.1 | async-start | bytes 1081344 | tf_op jit(solution)/shard_map/all_gather | solution.py:60
  67.8 211.0 %all-gather.9.cloned.1.call-start = ((), (), s32[]{:S(2)}) async-start(), calls=%async_computation.2 | async-start | bytes 1081344 | tf_op jit(solution)/shard_map/all_gather | solution.py:107
  67.8 0.7 copy-start.2
  68.5 0.7 copy-start.1
Sparse Core Ops, SparseCore 0:
  67.1 18.2 all-gather.10
  88.4 72.9 all-gather.6
  209.7 68.9 all-gather.8
where the time goes:
time: 368 us; the launch traced here: 366 us
  blocking collectives  143 us (39%)
  waiting for transfers between devices  112 us (30%)
  matrix products  77.2 us (21%)
  local copies, waits for them, and re-layouts  15 us (4%)
  between operations  13.3 us (4%)
    all_gather x1, waiting for transfers between devices, per_device(): vectors_all = lax.all_gather(vectors, TRAJ, axis=1, tiled=True)  74.4 us
    all_gather x1, blocking collectives, all_blocks(): blocks = lax.all_gather(blocks, axes[k], axis=0, tiled=True)  60.4 us
    all_gather x1, blocking collectives, sent_together(): out = lax.all_gather(both, axis, axis=dim, tiled=True)  47.4 us
    all_to_all x1, blocking collectives, copy_for_each(): return lax.all_to_all(copies, axis, split_axis=0, concat_axis=0, tiled=True)  35.2 us
    dot_general x16, matrix products, dense_kernel(): lax.dot_general(own, slab, (((0,), (0,)), ((), ())), precision=lax.Precis...  22.3 us
    dot_general x16, matrix products, pull_tile(): lax.dot_general(slab, own, (((0,), (0,)), ((), ())), precision=lax.Precis...  21.9 us
    all_gather x1, waiting for transfers between devices, per_device(): scaled_whole = lax.all_gather(scaled, TRAJ, axis=1, tiled=True)  20.6 us
    dot_general x16, matrix products, first_dense(): lax.dot_general(slab_vectors, weights, (((1,), (1,)), ((), ())), preferre...  16.5 us
  transfers between devices with their start and end apart: 3, of which 3 were waited for; matrix products, arithmetic and copies ran while one was open for 1% of the time, Pallas kernels for 0%

commit v1 on v0

--- a/solution.py
+++ b/solution.py
@@ -18,7 +18,19 @@
 def all_blocks(array, axes, turns):
     blocks = array[None]
     for k in turns:
-        blocks = lax.all_gather(blocks, axes[k], axis=0, tiled=True)
+
+        def space_serve(q_in, named_axis, k_dim):
+            return jnp.concatenate(
+                lax.all_to_all(
+                    jnp.stack(lax.axis_size(named_axis) * [q_in], 0),
+                    named_axis,
+                    split_axis=0,
+                    concat_axis=0,
+                ),
+                k_dim,
+            )
+
+        blocks = space_serve(blocks, axes[k], 0)
     block = [lax.axis_size(axes[k]) for k in reversed(turns)]
     blocks = blocks.reshape(*block, *array.shape)
     turned = sorted(range(len(turns)), key=lambda place: turns[len(turns) - 1 - place])

time: 368 us -> 311 us (0.85)
  blocking collectives: 143 us -> 87.3 us
  waiting for transfers between devices: 112 us -> 90.4 us
  starting transfers between devices: 0.08 us -> 18.3 us
    all_gather x1 -> x0, blocking collectives: 60.4 us -> none  [all_blocks(): blocks = lax.all_gather(blocks, axes[k], axis=0, tiled=True)]
    all_gather x1, waiting for transfers between devices: 74.4 us -> 44.6 us  [per_device(): vectors_all = lax.all_gather(vectors, TRAJ, axis=1, tiled=True)]
    all_to_all x0 -> x1, waiting for transfers between devices: none -> 24.6 us  [space_serve(): lax.all_to_all(jnp.stack(lax.axis_size(named_axis) * [q_in], 0), named_ax...]
    all_to_all x0 -> x1, starting transfers between devices: none -> 18.2 us  [space_serve(): lax.all_to_all(jnp.stack(lax.axis_size(named_axis) * [q_in], 0), named_ax...]
    all_gather x1 -> x0, waiting for transfers between devices: 16.1 us -> none  [all_blocks(): blocks = lax.all_gather(blocks, axes[k], axis=0, tiled=True)]
    all_to_all x0 -> x1, blocking collectives: none -> 4.58 us  [space_serve(): lax.all_to_all(jnp.stack(lax.axis_size(named_axis) * [q_in], 0), named_ax...]
where the time goes in v1:
time: 311 us; the launch traced here: 309 us
  waiting for transfers between devices  90.4 us (29%)
  blocking collectives  87.3 us (28%)
  matrix products  77.2 us (25%)
  starting transfers between devices  18.3 us (6%)
  local copies, waits for them, and re-layouts  16.4 us (5%)
  between operations  13.6 us (4%)
    all_gather x1, blocking collectives, sent_together(): out = lax.all_gather(both, axis, axis=dim, tiled=True)  47.5 us
    all_gather x1, waiting for transfers between devices, per_device(): vectors_all = lax.all_gather(vectors, TRAJ, axis=1, tiled=True)  44.6 us
    all_to_all x1, blocking collectives, copy_for_each(): return lax.all_to_all(copies, axis, split_axis=0, concat_axis=0, tiled=True)  35.2 us
    all_to_all x1, waiting for transfers between devices, space_serve(): lax.all_to_all(jnp.stack(lax.axis_size(named_axis) * [q_in], 0), named_ax...  24.6 us
    dot_general x16, matrix products, dense_kernel(): lax.dot_general(own, slab, (((0,), (0,)), ((), ())), precision=lax.Precis...  22.3 us
    dot_general x16, matrix products, pull_tile(): lax.dot_general(slab, own, (((0,), (0,)), ((), ())), precision=lax.Precis...  21.9 us
    all_gather x1, waiting for transfers between devices, per_device(): scaled_whole = lax.all_gather(scaled, TRAJ, axis=1, tiled=True)  20.6 us
    all_to_all x1, starting transfers between devices, space_serve(): lax.all_to_all(jnp.stack(lax.axis_size(named_axis) * [q_in], 0), named_ax...  18.2 us
  transfers between devices with their start and end apart: 3, of which 3 were waited for; matrix products, arithmetic and copies ran while one was open for 1% of the time, Pallas kernels for 0%

profile of v1, /device:TPU:8, one launch (start us, length us, event | category | flops | bytes accessed | tf_op | source)
XLA Modules:
  0.0 308.5 jit_solution(9189581458818021711)
XLA Ops:
  6.5 1.6 stack.6
  8.2 18.2 %all-to-all-start = ((f32[16,1,1,32,256]{4,3,2,1,0:T(8,128)}), f32[16,1,1,32,256]{4,3,2,1,0:T(8,128)S(1)}, u32[]{:S(2)}, u32[]{:S(2)}) async-start(f32[16,1,1,32,256]{4,3,2,1,0:T(8,128)} %stack.6), calls=%async_computation | async-start | bytes 1048576 | tf_op jit(solution)/shard_map/all_to_all | solution.py:24
  28.6 24.6 %all-to-all-done = f32[16,1,1,32,256]{4,3,2,1,0:T(8,128)S(1)} async-done(((f32[16,1,1,32,256]{4,3,2,1,0:T(8,128)}), f32[16,1,1,32,256]{4,3,2,1,0:T(8,128)S(1)}, u32[]{:S(2)}, u32[]{:S(2)}) %all-to-all-start) | async-done | bytes 524320 | tf_op jit(solution)/shard_map/all_to_all | solution.py:24
  54.0 4.6 %all_to_all.15 = f32[2,16,1,32,256]{4,1,3,2,0:T(8,128)S(1)} all-to-all(f32[2,16,1,32,256]{4,1,3,2,0:T(8,128)S(1)} %copy.22), channel_id=1, replica_groups=mesh['traj_0'=4,'traj_1'=4,'traj_2'=2,'tm'=16] {'traj_2'}, dimensions={0} | all-to-all | bytes 2097152 | tf_op jit(solution)/shard_map/all_to_all | solution.py:24
  59.4 44.6 %all-gather.4.cloned.1.call-done = bf16[64,8192]{1,0:T(8,128)(2,1)} async-done(((bf16[64,256]{1,0:T(8,128)(2,1)}), bf16[64,8192]{1,0:T(8,128)(2,1)}) %all-gather.4.cloned.1.call-update) | async-done | bytes 1048592 | tf_op jit(solution)/shard_map/all_gather | solution.py:72
  104.0 47.5 %while.34 = (s32[]{:T(128)}, f32[256]{0:T(256)S(1)}, f32[64,256]{1,0:T(8,128)S(1)}, f32[2,64]{1,0:T(2,128)S(1)}, f32[256]{0:T(256)S(1)}, /*index=5*/f32[8192]{0:...) while((s32[]{:T(128)}, f32[256]{0:T(256)S(1)}, ...), condition=%wide.region_6.7_spmd.clone, body=%wide.region_4.0_spmd.clone.sunk | while | flops 68190488 | bytes 1879617 | solution.py:108
  104.5 1.4 fusion.42
  105.9 1.0 convolution_add_fusion.4
  107.4 1.4 fusion.42
  108.8 1.0 convolution_add_fusion.4
  110.4 1.4 fusion.42
  111.8 1.0 convolution_add_fusion.4
  113.4 1.4 fusion.42
  116.4 1.4 fusion.42
  117.8 1.0 convolution_add_fusion.4
  119.3 1.4 fusion.42
  122.3 1.4 fusion.42
  123.7 1.0 convolution_add_fusion.4
  125.3 1.4 fusion.42
  128.2 1.4 fusion.42
  129.6 1.0 convolution_add_fusion.4
  131.2 1.4 fusion.42
  134.2 1.4 fusion.42
  135.6 1.0 convolution_add_fusion.4
  137.1 1.4 fusion.42
  140.1 1.4 fusion.42
  141.5 1.0 convolution_add_fusion.4
  143.1 1.4 fusion.42
  146.0 1.4 fusion.42
  147.4 1.0 convolution_add_fusion.4
  149.0 1.4 fusion.42
  152.3 47.5 %all-gather = s32[32,2,25]{2,1,0:T(2,128)S(1)} all-gather(s32[1,2,25]{2,1,0:T(2,128)S(1)} %add_bitcast_fusion), channel_id=1, replica_groups=mesh['traj_0'=4,'traj_1'=4,'traj_2'=2,'tm'=16] {'traj_0','traj_1','traj_2'}, dimensions={0}, use_global_device_ids=true | all-gather | bytes 6600 | tf_op jit(solution)/shard_map/all_gather | solution.py:49
  200.7 20.6 %all-gather.6.cloned.1.call-done = bf16[64,8192]{1,0:T(8,128)(2,1)} async-done(((bf16[64,256]{1,0:T(8,128)(2,1)}), bf16[64,8192]{1,0:T(8,128)(2,1)}) %all-gather.6.cloned.1.call-update) | async-done | bytes 1048592 | tf_op jit(solution)/shard_map/all_gather | solution.py:119
  221.3 44.3 %while.35 = (s32[]{:T(128)}, f32[64,256]{1,0:T(8,128)S(1)}, bf16[64,8192]{1,0:T(8,128)(2,1)}, f32[64,2]{1,0:T(8,128)S(1)}, f32[8192]{0:T(1024)S(1)}, /*index=5*/...) while((s32[]{:T(128)}, f32[64,256]{1,0:T(8,128)S(1)}, ...), condition=%wide.region_8.9_spmd.clone, body=%wide.region_7.8_spmd.clone.sunk | while | flops 68059160 | bytes 1875448 | solution.py:137
  221.6 1.4 fusion.47
  223.0 1.0 convolution_add_fusion.5
  224.4 1.4 fusion.47
  225.8 1.0 convolution_add_fusion.5
  227.2 1.4 fusion.47
  228.5 1.0 convolution_add_fusion.5
  229.9 1.4 fusion.47
  231.3 1.0 convolution_add_fusion.5
  232.7 1.4 fusion.47
  234.1 1.0 convolution_add_fusion.5
  235.5 1.4 fusion.47
  236.9 1.0 convolution_add_fusion.5
  238.3 1.4 fusion.47
  239.6 1.0 convolution_add_fusion.5
  241.0 1.4 fusion.47
  243.8 1.4 fusion.47
  245.2 1.0 convolution_add_fusion.5
  246.6 1.4 fusion.47
  248.0 1.0 convolution_add_fusion.5
  249.4 1.4 fusion.47
  250.7 1.0 convolution_add_fusion.5
  252.1 1.4 fusion.47
  253.5 1.0 convolution_add_fusion.5
  254.9 1.4 fusion.47
  256.3 1.0 convolution_add_fusion.5
  257.7 1.4 fusion.47
  260.5 1.4 fusion.47
  261.8 1.0 convolution_add_fusion.5
  263.2 1.4 fusion.47
  265.8 35.2 %all_to_all.16 = f32[16,64,256]{2,1,0:T(8,128)S(1)} all-to-all(f32[16,64,256]{2,1,0:T(8,128)S(1)} %broadcast_in_dim.33), channel_id=1, replica_groups=mesh['traj_0'=4,'traj_1'=4,'traj_2'=2,'tm'=16] {'tm'}, dimensions={0} | all-to-all | bytes 2097152 | tf_op jit(solution)/shard_map/all_to_all | solution.py:56
  (172 shorter events, 28.7 us)
Async XLA Ops:
  8.2 45.1 %all-to-all-start = ((f32[16,1,1,32,256]{4,3,2,1,0:T(8,128)}), f32[16,1,1,32,256]{4,3,2,1,0:T(8,128)S(1)}, u32[]{:S(2)}, u32[]{:S(2)}) async-start(f32[16,1,1,32,256]{4,3,2,1,0:T(8,128)} %stack.6), calls=%async_computation | async-start | bytes 1048576 | tf_op jit(solution)/shard_map/all_to_all | solution.py:24
  26.3 2.2 copy-start
  26.4 77.7 %all-gather.4.cloned.1.call-start = ((), (), s32[]{:S(2)}) async-start(), calls=%async_computation.3 | async-start | bytes 1081344 | tf_op jit(solution)/shard_map/all_gather | solution.py:72
  27.1 194.2 %all-gather.6.cloned.1.call-start = ((), (), s32[]{:S(2)}) async-start(), calls=%async_computation.4 | async-start | bytes 1081344 | tf_op jit(solution)/shard_map/all_gather | solution.py:119
  27.1 0.7 copy-start.2
  27.8 0.7 copy-start.1
Sparse Core Ops, SparseCore 0:
  30.2 73.7 all-gather.3
  152.3 69.0 all-gather.5
